TPU v7x, 128 devices: a whole 4x4x4 slice. The times are simulated.
128 devices in a mesh: blk: 32 (over z, y, x_hi), narrow: 4 (over x_lo, core).
Axes of the slice: x: 4 (x_hi: 2, x_lo: 2; x = x_hi * 2 + x_lo), y: 4, z: 4, core: 2. Of those that a mesh axis runs over, the one named last changes fastest.
Arguments:
- tokens: bfloat16 [16384, 1536], P(('blk', 'narrow')), may hold values from -6 to 6
- segments: int32 [16384], P(('blk', 'narrow')), may hold values from 0 to 15, never falling along the last dimension, each value on 1 to 2000 neighbouring positions
- attn_gain: float32 [1536], replicated, may hold values from 0.5 to 1.5
- w_query: bfloat16 [1536, 1536], P('blk', 'narrow'), may hold values from -0.15625 to 0.15625
- key_projection_weight: bfloat16 [1536, 512], P('blk', 'narrow'), may hold values from -0.15625 to 0.15625
- value_projection_weight: bfloat16 [1536, 512], P('blk', 'narrow'), may hold values from -0.15625 to 0.15625
- query_gain: float32 [64], replicated, may hold values from 0.1 to 1.9
- key_gain: float32 [64], replicated, may hold values from 0.1 to 1.9
- w_out: bfloat16 [1536, 1536], P('narrow', 'blk'), may hold values from -1.75 to 1.75
- ffn_gain: float32 [1536], replicated, may hold values from 0.5 to 1.5
- w_gate: bfloat16 [1536, 6912], P('blk', 'narrow'), may hold values from -0.15625 to 0.15625
- w_up: bfloat16 [1536, 6912], P('blk', 'narrow'), may hold values from -0.15625 to 0.15625
- w_down: bfloat16 [6912, 1536], P('narrow', 'blk'), may hold values from -0.078125 to 0.078125
- out_grad: bfloat16 [16384, 1536], P(('blk', 'narrow')), may hold values from -6 to 6
Outputs:
- result: bfloat16 [16384, 1536], P(('blk', 'narrow'))
- grad_tokens: bfloat16 [16384, 1536], P(('blk', 'narrow'))
- grad_attn_gain: float32 [1536], replicated
- grad_query: float32 [1536, 1536], P('blk', 'narrow')
- grad_key: float32 [1536, 512], P('blk', 'narrow')
- grad_value: float32 [1536, 512], P('blk', 'narrow')
- grad_query_gain: float32 [64], replicated
- grad_key_gain: float32 [64], replicated
- grad_out: float32 [1536, 1536], P('narrow', 'blk')
- grad_ffn_gain: float32 [1536], replicated
- grad_gate: float32 [1536, 6912], P('blk', 'narrow')
- grad_up: float32 [1536, 6912], P('blk', 'narrow')
- grad_down: float32 [6912, 1536], P('narrow', 'blk')
Inputs may be any that keep to these rules, and one draw needn't show every extreme that they name: `segments`: segment numbers never fall along the sequence; each document holds 1 to 2000 tokens, one exactly 2000.
All inputs are finite; a program needn't handle non-finite values.
Results may differ from a plain program's by a relative error of at most 0.02.
Values may be sent and summed in bfloat16 or wider, within the bound.
A program may use at most 192 MiB of HBM per device.

v0:
```python
from functools import partial

import jax
import jax.numpy as jnp
from jax import lax
from jax.sharding import Mesh
from jax.sharding import PartitionSpec as P

DOC_MOST = 2000
BLK = ("blk_0", "blk_1", "blk_2")
BLK_NARROW = ("blk_0", "blk_1", "blk_2", "narrow")


EPS = 1e-05
THETA = 1000000.0
NEG = -1e30


def joined_along(pieces, dim):
    pieces = jnp.moveaxis(pieces, 0, dim)
    lengths = pieces.shape
    return pieces.reshape(*lengths[:dim], lengths[dim] * lengths[dim + 1], *lengths[dim + 2 :])


def from_everyone(x, axis):
    copies = jnp.broadcast_to(x, (lax.axis_size(axis), *x.shape))
    return lax.all_to_all(copies, axis, split_axis=0, concat_axis=0, tiled=True)


def gathered_copies(x, axis, dim):
    return joined_along(from_everyone(x, axis), dim)


def cut_along(x, dim, devices):
    before, after = (x.shape[:dim], x.shape[dim + 1 :])
    return jnp.moveaxis(x.reshape(*before, devices, -1, *after), dim, 0)


def sum_at_owner(x, axis, dim):
    devices = lax.axis_size(axis)
    pieces = lax.all_to_all(cut_along(x, dim, devices), axis, 0, 0, tiled=True)
    return jnp.sum(pieces, axis=0)


def sum_at_owner_2(x, axis, dim):
    devices = lax.axis_size(axis)
    pieces = lax.all_to_all(cut_along(x, dim, devices), axis, 0, 0, tiled=True)
    return jnp.sum(pieces.astype(jnp.float32), axis=0)


def rows_first(arrays, axis, dims):
    turned = [jnp.moveaxis(a, dim, 0) for a, dim in zip(arrays, dims)]
    both = jnp.concatenate([t.reshape(len(t), -1) for t in turned], axis=1)
    whole, at, gathered = (lax.all_gather(both, axis, axis=0, tiled=True), 0, [])
    for t, dim in zip(turned, dims):
        slab = whole[:, at : at + t[0].size].reshape(-1, *t.shape[1:])
        gathered.append(jnp.moveaxis(slab, 0, dim))
        at += t[0].size
    return tuple(gathered)


def passed_along(block, axis, distance):
    devices = range(lax.axis_size(axis))
    route = [(i - distance, i) for i in devices if i - distance in devices]
    return lax.ppermute(block, axis, route)


def sum_by_axis(terms, axes):
    running = terms.astype(jnp.bfloat16)
    for axis in axes:
        running = lax.psum_scatter(running, axis, scatter_dimension=0, tiled=True)
    return running.astype(jnp.float32)


def over_pieces(x, axis):
    pieces = lax.all_gather(x, axis)
    return pieces.sum(axis=0)


def rms_scale(values, gain):
    inverse = lax.rsqrt(jnp.mean(values * values, axis=-1, keepdims=True) + EPS)
    return values * inverse * gain


def rotate(values, positions):
    half = values.shape[-1] // 2
    steps = jnp.arange(half, dtype=jnp.float32) * (2.0 / values.shape[-1])
    freqs = jnp.exp(-jnp.log(THETA) * steps)
    angles = positions[:, None] * freqs[None, :]
    cosine = jnp.cos(angles)[:, None, :]
    sine = jnp.sin(angles)[:, None, :]
    first_index = values[..., :half]
    second = values[..., half:]
    return jnp.concatenate(
        [first_index * cosine - second * sine, second * cosine + first_index * sine], axis=-1
    )


def head_prepare(raw, gain, positions):
    return rotate(rms_scale(raw, gain), positions)


def gather_rows(values):
    return gathered_copies(values, "narrow", 0)


def branch_rows(values):
    return sum_at_owner(values, "narrow", 0)


def input_rows(values):
    return sum_at_owner_2(values.astype(jnp.bfloat16), "narrow", 0)


def on_device(
    tokens,
    segments,
    attn_gain,
    w_query,
    key_projection_weight,
    value_projection_weight,
    query_gain,
    key_gain,
    w_out,
    ffn_gain,
    w_gate,
    w_up,
    w_down,
    out_grad,
):
    single_float = jnp.float32
    bf16 = jnp.bfloat16
    narrow_count = lax.axis_size("narrow")
    blk_count = lax.axis_size(BLK)
    rows = tokens.shape[0] * narrow_count
    head_size = query_gain.shape[0]
    q_heads = w_query.shape[1] // head_size
    kv_heads = key_projection_weight.shape[1] // head_size
    query_group = q_heads // kv_heads
    scale = head_size ** (-0.5)
    reach = min((DOC_MOST - 2) // rows + 1, blk_count - 1)
    block = lax.axis_index(BLK)
    seg_query = gathered_copies(segments, "narrow", 0)
    start = block * rows
    positions = start + jnp.arange(rows, dtype=jnp.int32)
    float_pos = positions.astype(single_float)
    segment_list = [seg_query]

    def key_info(steps_back):
        key_block = block - steps_back
        seg_key = segment_list[steps_back]
        key_pos = key_block * rows + jnp.arange(rows, dtype=jnp.int32)
        allowed = (
            (seg_query[:, None] == seg_key[None, :])
            & (key_pos[None, :] <= positions[:, None])
            & (key_block >= 0)
        )
        needed = (key_block >= 0) & (seg_key[rows - 1] == seg_query[0])
        return (allowed, needed)

    tokens_f = tokens.astype(single_float)
    block_one = gather_rows(rms_scale(tokens_f, attn_gain).astype(bf16))
    wq_all, wk_all, wv_all, wo_all = rows_first(
        (w_query, key_projection_weight, value_projection_weight, w_out), BLK, (0, 0, 0, 1)
    )
    q_raw = jnp.dot(block_one, wq_all, preferred_element_type=single_float).reshape(
        rows, q_heads, head_size
    )
    key_unrotated = jnp.dot(block_one, wk_all, preferred_element_type=single_float).reshape(
        rows, kv_heads, head_size
    )
    v_now = (
        jnp.dot(block_one, wv_all, preferred_element_type=single_float)
        .astype(bf16)
        .reshape(rows, kv_heads, head_size)
    )
    q_now = (
        head_prepare(q_raw, query_gain, float_pos)
        .astype(bf16)
        .reshape(rows, kv_heads, query_group, head_size)
    )
    k_now = head_prepare(key_unrotated, key_gain, float_pos).astype(bf16)
    key_list = [k_now]
    value_list = [v_now]
    for steps_back in range(1, reach + 1):
        k_next, v_next = passed_along((key_list[-1], value_list[-1]), BLK, 1)
        key_list.append(k_next)
        value_list.append(v_next)
        segment_list.append(passed_along(segment_list[-1], BLK, 1))
    infos = [key_info(steps_back) for steps_back in range(reach + 1)]

    def scores(steps_back):
        raw = (
            jnp.einsum(
                "qhgd,khd->hgqk", q_now, key_list[steps_back], preferred_element_type=single_float
            )
            * scale
        )
        return jnp.where(infos[steps_back][0][None, None], raw, NEG)

    def guarded(steps_back, compute, skipped, state):
        if steps_back == 0:
            return compute(state)
        return lax.cond(infos[steps_back][1], compute, skipped, state)

    first_scores = scores(0)
    top = jnp.max(first_scores, axis=-1)
    total = jnp.sum(jnp.exp(first_scores - top[..., None]), axis=-1)

    def stats_step(steps_back, state):
        old_top, old_total = state
        current = scores(steps_back)
        new_top = jnp.maximum(old_top, jnp.max(current, axis=-1))
        new_total = old_total * jnp.exp(old_top - new_top) + jnp.sum(
            jnp.exp(current - new_top[..., None]), axis=-1
        )
        return (new_top, new_total)

    for steps_back in range(1, reach + 1):
        top, total = guarded(
            steps_back, partial(stats_step, steps_back), lambda state: state, (top, total)
        )

    def probs(steps_back):
        return jnp.exp(scores(steps_back) - top[..., None]) / total[..., None]

    def output_step(steps_back, acc):
        weights = probs(steps_back).astype(bf16)
        return acc + jnp.einsum(
            "hgqk,khd->qhgd", weights, value_list[steps_back], preferred_element_type=single_float
        )

    out_acc = jnp.zeros((rows, kv_heads, query_group, head_size), single_float)
    for steps_back in range(reach + 1):
        out_acc = guarded(
            steps_back, partial(output_step, steps_back), lambda state: state, out_acc
        )
    out_block = out_acc.reshape(rows, q_heads * head_size).astype(bf16)
    attn_branch = branch_rows(jnp.dot(out_block, wo_all, preferred_element_type=single_float))
    mid = tokens_f + attn_branch
    block_two = gather_rows(rms_scale(mid, ffn_gain).astype(bf16))
    wg_all, wu_all, wd_all = rows_first((w_gate, w_up, w_down), BLK, (0, 0, 1))
    gate = jnp.dot(block_two, wg_all, preferred_element_type=single_float)
    up = jnp.dot(block_two, wu_all, preferred_element_type=single_float)
    sigmoid = jax.nn.sigmoid(gate)
    swish = gate * sigmoid
    hidden = (swish * up).astype(bf16)
    ffn_branch = branch_rows(jnp.dot(hidden, wd_all, preferred_element_type=single_float))
    result = (mid + ffn_branch).astype(bf16)
    out_rows = gather_rows(out_grad)
    d_hidden = jnp.einsum("rd,fd->rf", out_rows, wd_all, preferred_element_type=single_float)
    d_gate = (d_hidden * up * sigmoid * (1.0 + gate * (1.0 - sigmoid))).astype(bf16)
    d_up = (d_hidden * swish).astype(bf16)
    d_normed_two = input_rows(
        jnp.einsum("rf,df->rd", d_gate, wg_all, preferred_element_type=single_float)
        + jnp.einsum("rf,df->rd", d_up, wu_all, preferred_element_type=single_float)
    )
    grad_pair = jnp.concatenate([d_gate, d_up], axis=1)
    ff_local = w_gate.shape[1]
    left = block_two
    right = out_rows
    inner = jnp.einsum("rc,rj->cj", left, grad_pair, preferred_element_type=single_float)
    outer = jnp.einsum("rc,rj->cj", right, hidden, preferred_element_type=single_float)
    ffn_grads = sum_by_axis(jnp.concatenate([inner, outer], axis=1), BLK)
    _, norm_two_back = jax.vjp(rms_scale, mid, ffn_gain)
    d_mid_norm, d_ffn_gain = norm_two_back(d_normed_two)
    d_mid = out_grad.astype(single_float) + d_mid_norm
    mid_rows = gather_rows(d_mid.astype(bf16))
    d_out = (
        jnp.einsum("rd,jd->rj", mid_rows, wo_all, preferred_element_type=single_float)
        .astype(bf16)
        .reshape(rows, kv_heads, query_group, head_size)
    )

    def delta_step(steps_back, acc):
        d_probs = jnp.einsum(
            "qhgd,khd->hgqk", d_out, value_list[steps_back], preferred_element_type=single_float
        )
        return acc + jnp.sum(probs(steps_back) * d_probs, axis=-1)

    delta = jnp.zeros((kv_heads, query_group, rows), single_float)
    for steps_back in range(reach + 1):
        delta = guarded(steps_back, partial(delta_step, steps_back), lambda state: state, delta)

    def back_step(steps_back, state):
        d_acc, unused_k, unused_v = state
        current = probs(steps_back)
        d_probs = jnp.einsum(
            "qhgd,khd->hgqk", d_out, value_list[steps_back], preferred_element_type=single_float
        )
        d_scores = (current * (d_probs - delta[..., None])).astype(bf16)
        d_acc = (
            d_acc
            + jnp.einsum(
                "hgqk,khd->qhgd",
                d_scores,
                key_list[steps_back],
                preferred_element_type=single_float,
            )
            * scale
        )
        d_key = (
            jnp.einsum("hgqk,qhgd->khd", d_scores, q_now, preferred_element_type=single_float)
            * scale
        )
        d_value = jnp.einsum(
            "hgqk,qhgd->khd", current.astype(bf16), d_out, preferred_element_type=single_float
        )
        return (d_acc, d_key, d_value)

    def back_skipped(state):
        d_acc, unused_k, unused_v = state
        return (d_acc, jnp.zeros_like(unused_k), jnp.zeros_like(unused_v))

    d_query = jnp.zeros((rows, kv_heads, query_group, head_size), single_float)
    empty_kv = jnp.zeros((rows, kv_heads, head_size), single_float)
    grad_k = empty_kv
    grad_v = empty_kv
    for steps_back in range(reach, -1, -1):
        d_query, part_k, part_v = guarded(
            steps_back, partial(back_step, steps_back), back_skipped, (d_query, empty_kv, empty_kv)
        )
        if steps_back == reach:
            grad_k, grad_v = (part_k, part_v)
        else:
            moved_k, moved_v = (
                passed_along(grad_k.astype(jnp.bfloat16), BLK, -1).astype(grad_k.dtype),
                passed_along(grad_v.astype(jnp.bfloat16), BLK, -1).astype(grad_v.dtype),
            )
            grad_k = moved_k + part_k
            grad_v = moved_v + part_v
    dq_used = d_query.astype(bf16).astype(single_float).reshape(rows, q_heads, head_size)
    dk_used = grad_k.astype(bf16).astype(single_float)
    _, q_back = jax.vjp(lambda raw, gain: head_prepare(raw, gain, float_pos), q_raw, query_gain)
    dq_raw, d_query_gain = q_back(dq_used)
    _, k_back = jax.vjp(
        lambda raw, gain: head_prepare(raw, gain, float_pos), key_unrotated, key_gain
    )
    dk_raw, d_key_gain = k_back(dk_used)
    dq_low = dq_raw.reshape(rows, q_heads * head_size).astype(bf16)
    dk_low = dk_raw.reshape(rows, kv_heads * head_size).astype(bf16)
    dv_low = grad_v.reshape(rows, kv_heads * head_size).astype(bf16)
    d_normed_one = input_rows(
        jnp.einsum("rj,dj->rd", dq_low, wq_all, preferred_element_type=single_float)
        + jnp.einsum("rj,dj->rd", dk_low, wk_all, preferred_element_type=single_float)
        + jnp.einsum("rj,dj->rd", dv_low, wv_all, preferred_element_type=single_float)
    )
    grad_proj = jnp.concatenate([dq_low, dk_low, dv_low], axis=1)
    left = block_one
    right = mid_rows
    inner = jnp.einsum("rc,rj->cj", left, grad_proj, preferred_element_type=single_float)
    outer = jnp.einsum("rc,rj->cj", right, out_block, preferred_element_type=single_float)
    attn_grads = lax.psum_scatter(
        jnp.concatenate([inner, outer], axis=1).astype(jnp.bfloat16),
        BLK,
        scatter_dimension=0,
        tiled=True,
    ).astype(jnp.float32)
    _, norm_one_back = jax.vjp(rms_scale, tokens_f, attn_gain)
    d_tok_norm, d_attn_gain = norm_one_back(d_normed_one)
    grad_tokens = (d_mid + d_tok_norm).astype(bf16)
    sum_attn, sum_query, sum_key, sum_ffn = (
        over_pieces(d_attn_gain, BLK_NARROW),
        over_pieces(d_query_gain, BLK_NARROW),
        over_pieces(d_key_gain, BLK_NARROW),
        over_pieces(d_ffn_gain, BLK_NARROW),
    )
    q_width = w_query.shape[1]
    k_width = key_projection_weight.shape[1]
    grad_query = attn_grads[:, :q_width]
    grad_key = attn_grads[:, q_width : q_width + k_width]
    grad_value = attn_grads[:, q_width + k_width : q_width + 2 * k_width]
    grad_out = attn_grads[:, q_width + 2 * k_width :].T
    grad_gate = ffn_grads[:, :ff_local]
    grad_up = ffn_grads[:, ff_local : 2 * ff_local]
    grad_down = ffn_grads[:, 2 * ff_local :].T
    return (
        result,
        grad_tokens,
        sum_attn,
        grad_query,
        grad_key,
        grad_value,
        sum_query,
        sum_key,
        grad_out,
        sum_ffn,
        grad_gate,
        grad_up,
        grad_down,
    )


def solution(mesh):
    finer = Mesh(
        mesh.devices.reshape(4, 4, 2, mesh.shape["narrow"]), ("blk_0", "blk_1", "blk_2", "narrow")
    )
    in_specs = (
        P(BLK_NARROW, None),
        P(BLK_NARROW),
        P(),
        P(BLK, "narrow"),
        P(BLK, "narrow"),
        P(BLK, "narrow"),
        P(),
        P(),
        P("narrow", BLK),
        P(),
        P(BLK, "narrow"),
        P(BLK, "narrow"),
        P("narrow", BLK),
        P(BLK_NARROW, None),
    )
    out_specs = (
        P(BLK_NARROW, None),
        P(BLK_NARROW, None),
        P(),
        P(BLK, "narrow"),
        P(BLK, "narrow"),
        P(BLK, "narrow"),
        P(),
        P(),
        P("narrow", BLK),
        P(),
        P(BLK, "narrow"),
        P(BLK, "narrow"),
        P("narrow", BLK),
    )
    return jax.shard_map(
        on_device, mesh=finer, in_specs=in_specs, out_specs=out_specs, check_vma=False
    )
```

profile of v0, /device:TPU:1, one launch (start us, length us, event | category | flops | bytes accessed | tf_op | source)
XLA Modules:
  0.0 992.5 jit_solution(8303599174737283539)
XLA Ops:
  31.1 12.8 %collective-permute-done = s32[512]{0:T(512)S(1)} collective-permute-done((s32[512]{0:T(512)S(1)}, s32[512]{0:T(512)S(1)}, u32[]{:S(2)}, u32[]{:S(2)}) %collective-permute-start) | collective-permute-done | bytes 2080 | tf_op jit(solution)/shard_map/ppermute | solution.py:65
  73.1 16.0 %all-gather.9.cloned.1.call-done = bf16[1536,1024]{1,0:T(8,128)(2,1)} async-done(((bf16[48,1024]{1,0:T(8,128)(2,1)}), bf16[1536,1024]{1,0:T(8,128)(2,1)}) %all-gather.9.cloned.1.call-update) | async-done | bytes 3145744 | tf_op jit(solution)/shard_map/all_gather | solution.py:54
  137.2 8.9 collective-permute-start.11
  158.7 81.6 %all_to_all.46 = f32[4,128,1536]{2,1,0:T(8,128)S(1)} all-to-all(f32[4,128,1536]{2,1,0:T(8,128)S(1)} %fusion.225), channel_id=1, replica_groups=mesh['blk_0'=4,'blk_1'=4,'blk_2'=2,'narrow'=4] {'narrow'}, dimensions={0} | all-to-all | bytes 6291456 | tf_op jit(solution)/shard_map/all_to_all | solution.py:41
  249.4 31.9 %all-to-all-done.5 = bf16[4,128,1536]{2,1,0:T(8,128)(2,1)} async-done(((bf16[4,128,1536]{2,1,0:T(8,128)(2,1)}), bf16[4,128,1536]{2,1,0:T(8,128)(2,1)}, u32[]{:S(2)}, u32[]{:S(2)}) %all-to-all-start.5) | async-done | bytes 1572896 | tf_op jit(solution)/shard_map/all_to_all | solution.py:27
  286.7 10.7 %all-gather.11.cloned.1.call-done = bf16[1536,5184]{1,0:T(8,128)(2,1)} async-done(((bf16[48,5184]{1,0:T(8,128)(2,1)}), bf16[1536,5184]{1,0:T(8,128)(2,1)}) %all-gather.11.cloned.1.call-update) | async-done | bytes 15925264 | tf_op jit(solution)/shard_map/all_gather | solution.py:54
  297.4 8.0 fusion.187
  311.4 10.9 %fusion.205 = (bf16[512,1728]{0,1:T(8,128)(2,1)}, bf16[512,1728]{0,1:T(8,128)(2,1)}, bf16[512,1728]{0,1:T(8,128)(2,1)S(1)}) fusion(f32[1728,512]{1,0:T(8,128)S(1)} %copy-done.105, f32[512,1728]{0,1:T(8,128)S(1)} %fusion.197, bf16[512,1536]{1,0:T(8,128)(2,1)S(1)} %bitcast.668, bf16[1536,5184]{1,0:T(8,128)(2,1)} %all-gather.11.cloned.1.call-done), kind=kOutput, calls=%fused_computation.219 | convolution fusion | flops 2731180032 | bytes 19464192 | tf_op jit(solution)/shard_map/dot_general | solution.py:244
  329.5 7.9 copy.150
  337.5 8.5 convolution_convert_fusion
  352.6 7.7 fusion.191
  366.0 23.1 %all_to_all.47 = bf16[4,128,1536]{2,1,0:T(8,128)(2,1)S(1)} all-to-all(bf16[4,128,1536]{2,1,0:T(8,128)(2,1)S(1)} %bitcast.670), channel_id=1, replica_groups=mesh['blk_0'=4,'blk_1'=4,'blk_2'=2,'narrow'=4] {'narrow'}, dimensions={0} | all-to-all | bytes 3145728 | tf_op jit(solution)/shard_map/all_to_all | solution.py:47
  395.9 19.3 %all-to-all-done.7 = bf16[4,128,1536]{2,1,0:T(8,128)(2,1)S(1)} async-done(((bf16[4,128,1536]{2,1,0:T(8,128)(2,1)}), bf16[4,128,1536]{2,1,0:T(8,128)(2,1)S(1)}, u32[]{:S(2)}, u32[]{:S(2)}) %all-to-all-start.7) | async-done | bytes 1572896 | tf_op jit(solution)/shard_map/all_to_all | solution.py:27
  446.8 12.9 %collective-permute-done.12 = bf16[512,2,64]{0,2,1:T(8,128)(2,1)S(1)} collective-permute-done((bf16[512,2,64]{0,2,1:T(8,128)(2,1)}, bf16[512,2,64]{0,2,1:T(8,128)(2,1)S(1)}, u32[]{:S(2)}, u32[]{:S(2)}) %collective-permute-start.12) | collective-permute-done | bytes 131104 | tf_op jit(solution)/shard_map/ppermute | solution.py:65
  469.1 6.8 collective-permute-done.14
  491.0 14.5 %reduce-scatter.7.cloned.1.call-done = bf16[384,5184]{1,0:T(8,128)(2,1)} async-done(((bf16[1536,5184]{1,0:T(8,128)(2,1)}), bf16[384,5184]{1,0:T(8,128)(2,1)}) %reduce-scatter.7.cloned.1.call-update) | async-done | bytes 3981328 | tf_op jit(solution)/shard_map/reduce_scatter | solution.py:71
  549.1 7.9 fusion.189
  556.9 8.4 all-to-all-start.4
  572.2 29.6 %all-to-all-done.4 = f32[4,128,1536]{2,1,0:T(8,128)S(1)} async-done(((f32[4,128,1536]{2,1,0:T(8,128)}), f32[4,128,1536]{2,1,0:T(8,128)S(1)}, u32[]{:S(2)}, u32[]{:S(2)}) %all-to-all-start.4) | async-done | bytes 3145760 | tf_op jit(solution)/shard_map/all_to_all | solution.py:41
  608.7 96.8 %all-gather.5 = f32[128,1,1536]{2,1,0:T(1,128)S(1)} all-gather(f32[1,1,1536]{2,1,0:T(1,128)S(1)} %reshape.403), channel_id=5, replica_groups=mesh['blk_0'=4,'blk_1'=4,'blk_2'=2,'narrow'=4] {'blk_0','blk_1','blk_2',..., dimensions={0}, use_global_device_ids=true | all-gather | bytes 792576 | tf_op jit(solution)/shard_map/all_gather | solution.py:76
  712.6 16.0 %reduce-scatter.9.cloned.1.call-done = bf16[96,5184]{1,0:T(8,128)(2,1)} async-done(((bf16[384,5184]{1,0:T(8,128)(2,1)}), bf16[96,5184]{1,0:T(8,128)(2,1)}) %reduce-scatter.9.cloned.1.call-update) | async-done | bytes 995344 | tf_op jit(solution)/shard_map/reduce_scatter | solution.py:71
  730.6 39.9 %all-gather.4 = f32[128,1,1536]{2,1,0:T(1,128)} all-gather(f32[1,1,1536]{2,1,0:T(1,128)S(1)} %reshape.401), channel_id=2, replica_groups=mesh['blk_0'=4,'blk_1'=4,'blk_2'=2,'narrow'=4] {'blk_0','blk_1','blk_2',..., dimensions={0}, use_global_device_ids=true | all-gather | bytes 792576 | tf_op jit(solution)/shard_map/all_gather | solution.py:76
  775.1 180.9 %reduce-scatter.13.cloned.1.call-done = bf16[48,1024]{1,0:T(8,128)(2,1)} async-done(((bf16[1536,1024]{1,0:T(8,128)(2,1)}), bf16[48,1024]{1,0:T(8,128)(2,1)}) %reduce-scatter.13.cloned.1.call-update) | async-done | bytes 98320
  960.1 21.4 %reduce-scatter.11.cloned.1.call-done = bf16[48,5184]{1,0:T(8,128)(2,1)} async-done(((bf16[96,5184]{1,0:T(8,128)(2,1)}), bf16[48,5184]{1,0:T(8,128)(2,1)}) %reduce-scatter.11.cloned.1.call-update) | async-done | bytes 497680 | tf_op jit(solution)/shard_map/reduce_scatter | solution.py:71
  (396 shorter events, 290.1 us)
Async XLA Ops:
  7.2 81.9 %all-gather.9.cloned.1.call-start = ((), (), s32[]{:S(2)}) async-start(), calls=%async_computation.13 | async-start | bytes 3244032 | tf_op jit(solution)/shard_map/all_gather | solution.py:54
  8.7 288.7 %all-gather.11.cloned.1.call-start = ((), (), s32[]{:S(2)}) async-start(), calls=%async_computation.14 | async-start | bytes 16625664 | tf_op jit(solution)/shard_map/all_gather | solution.py:54
  21.0 71.9 %all-to-all-start.1 = ((bf16[4,128,1536]{2,1,0:T(8,128)(2,1)}), bf16[4,128,1536]{2,1,0:T(8,128)(2,1)}, u32[]{:S(2)}, u32[]{:S(2)}) async-start(bf16[4,128,1536]{2,1,0:T(8,128)(2,1)} %broadcast_in_dim.289), calls=%async_computation.1 | async-start | bytes 3145728 | tf_op jit(solution)/shard_map/all_to_all | solution.py:27
  26.0 17.9 %collective-permute-start = (s32[512]{0:T(512)S(1)}, s32[512]{0:T(512)S(1)}, u32[]{:S(2)}, u32[]{:S(2)}) collective-permute-start(s32[512]{0:T(512)S(1)} %bitcast.682), channel_id=1, source_target_pairs={{0,4},{4,8},{8,12},{12,16},{16,20},{20,24},{24,28},{28,32},{32,36}... | collective-permute-start | bytes 6152 | tf_op jit(solution)/shard_map/ppermute | solution.py:65
  56.6 12.2 %collective-permute-start.3 = (s32[512]{0:T(512)S(1)}, s32[512]{0:T(512)S(1)}, u32[]{:S(2)}, u32[]{:S(2)}) collective-permute-start(s32[512]{0:T(512)S(1)} %collective-permute-done.2), channel_id=1, source_target_pairs={{0,4},{4,8},{8,12},{12,16},{16,20},{20,24},{24,28},{28,32},{32,36}... | collective-permute-start | bytes 6152 | tf_op jit(solution)/shard_map/ppermute | solution.py:65
  95.7 20.9 %collective-permute-start.8 = (bf16[512,2,64]{0,2,1:T(8,128)(2,1)}, bf16[512,2,64]{0,2,1:T(8,128)(2,1)}, u32[]{:S(2)}, u32[]{:S(2)}) collective-permute-start(bf16[512,2,64]{0,2,1:T(8,128)(2,1)} %bitcast.119), channel_id=1, source_target_pairs={{0,4},{4,8},{8,12},{12,16},{16,20},{20,24},{24,28},{28,32},{32,36}... | collective-permute-start | bytes 393224 | tf_op jit(solution)/shard_map/ppermute | solution.py:65
  102.8 12.0 %collective-permute-start.4 = (bf16[512,2,64]{0,2,1:T(8,128)(2,1)}, bf16[512,2,64]{0,2,1:T(8,128)(2,1)}, u32[]{:S(2)}, u32[]{:S(2)}) collective-permute-start(bf16[512,2,64]{0,2,1:T(8,128)(2,1)} %pad_maximum_fusion.3), channel_id=1, source_target_pairs={{0,4},{4,8},{8,12},{12,16},{16,20},{20,24},{24,28},{28,32},{32,36}... | collective-permute-start | bytes 393224 | tf_op jit(solution)/shard_map/ppermute | solution.py:65
  116.6 9.6 collective-permute-start.9
  122.7 9.4 collective-permute-start.6
  126.2 10.9 %collective-permute-start.10 = (bf16[512,2,64]{0,2,1:T(8,128)(2,1)}, bf16[512,2,64]{0,2,1:T(8,128)(2,1)}, u32[]{:S(2)}, u32[]{:S(2)}) collective-permute-start(bf16[512,2,64]{0,2,1:T(8,128)(2,1)} %collective-permute-done.9), channel_id=1, source_target_pairs={{0,4},{4,8},{8,12},{12,16},{16,20},{20,24},{24,28},{28,32},{32,36}... | collective-permute-start | bytes 393224 | tf_op jit(solution)/shard_map/ppermute | solution.py:65
  132.1 14.0 %collective-permute-start.7 = (bf16[512,2,64]{0,2,1:T(8,128)(2,1)}, bf16[512,2,64]{0,2,1:T(8,128)(2,1)}, u32[]{:S(2)}, u32[]{:S(2)}) collective-permute-start(bf16[512,2,64]{0,2,1:T(8,128)(2,1)} %collective-permute-done.6), channel_id=1, source_target_pairs={{0,4},{4,8},{8,12},{12,16},{16,20},{20,24},{24,28},{28,32},{32,36}... | collective-permute-start | bytes 393224 | tf_op jit(solution)/shard_map/ppermute | solution.py:65
  137.2 15.6 %collective-permute-start.11 = (bf16[512,2,64]{0,2,1:T(8,128)(2,1)}, bf16[512,2,64]{0,2,1:T(8,128)(2,1)}, u32[]{:S(2)}, u32[]{:S(2)}) collective-permute-start(bf16[512,2,64]{0,2,1:T(8,128)(2,1)} %collective-permute-done.10), channel_id=1, source_target_pairs={{0,4},{4,8},{8,12},{12,16},{16,20},{20,24},{24,28},{28,32},{32,36}... | collective-permute-start | bytes 393224 | tf_op jit(solution)/shard_map/ppermute | solution.py:65
  241.6 39.7 %all-to-all-start.5 = ((bf16[4,128,1536]{2,1,0:T(8,128)(2,1)}), bf16[4,128,1536]{2,1,0:T(8,128)(2,1)}, u32[]{:S(2)}, u32[]{:S(2)}) async-start(bf16[4,128,1536]{2,1,0:T(8,128)(2,1)} %broadcast_in_dim.293), calls=%async_computation.5 | async-start | bytes 3145728 | tf_op jit(solution)/shard_map/all_to_all | solution.py:27
  282.6 23.3 %all-to-all-start.3 = ((bf16[4,128,1536]{2,1,0:T(8,128)(2,1)}), bf16[4,128,1536]{2,1,0:T(8,128)(2,1)S(1)}, u32[]{:S(2)}, u32[]{:S(2)}) async-start(bf16[4,128,1536]{2,1,0:T(8,128)(2,1)} %broadcast_in_dim.292), calls=%async_computation.3 | async-start | bytes 3145728 | tf_op jit(solution)/shard_map/all_to_all | solution.py:27
  286.7 218.7 %reduce-scatter.7.cloned.1.call-start = ((), (), s32[]{:S(2)}) async-start(), calls=%async_computation.15 | async-start | bytes 20152320 | tf_op jit(solution)/shard_map/reduce_scatter | solution.py:71
  391.7 23.5 %all-to-all-start.7 = ((bf16[4,128,1536]{2,1,0:T(8,128)(2,1)}), bf16[4,128,1536]{2,1,0:T(8,128)(2,1)S(1)}, u32[]{:S(2)}, u32[]{:S(2)}) async-start(bf16[4,128,1536]{2,1,0:T(8,128)(2,1)} %broadcast_in_dim.295), calls=%async_computation.7 | async-start | bytes 3145728 | tf_op jit(solution)/shard_map/all_to_all | solution.py:27
  395.9 313.9 %all-reduce.9.cloned.1.call-start = ((), (), s32[]{:S(2)}) async-start(), calls=%async_computation.19 | async-start | bytes 131072
  438.5 21.3 %collective-permute-start.12 = (bf16[512,2,64]{0,2,1:T(8,128)(2,1)}, bf16[512,2,64]{0,2,1:T(8,128)(2,1)S(1)}, u32[]{:S(2)}, u32[]{:S(2)}) collective-permute-start(bf16[512,2,64]{0,2,1:T(8,128)(2,1)} %get-tuple-element.441), channel_id=1, source_target_pairs={{4,0},{8,4},{12,8},{16,12},{20,16},{24,20},{28,24},{32,28},{36,32}... | collective-permute-start | bytes 393224 | tf_op jit(solution)/shard_map/ppermute | solution.py:65
  476.6 8.6 collective-permute-start.15
  490.9 237.6 %reduce-scatter.9.cloned.1.call-start = ((), (), s32[]{:S(2)}) async-start(), calls=%async_computation.16 | async-start | bytes 5038080 | tf_op jit(solution)/shard_map/reduce_scatter | solution.py:71
  505.5 450.5 %reduce-scatter.13.cloned.1.call-start = ((), (), s32[]{:S(2)}) async-start(), calls=%async_computation.18 | async-start | bytes 3244032
  556.9 44.8 %all-to-all-start.4 = ((f32[4,128,1536]{2,1,0:T(8,128)}), f32[4,128,1536]{2,1,0:T(8,128)S(1)}, u32[]{:S(2)}, u32[]{:S(2)}) async-start(f32[4,128,1536]{2,1,0:T(8,128)} %bitcast.658), calls=%async_computation.4 | async-start | bytes 6291456 | tf_op jit(solution)/shard_map/all_to_all | solution.py:41
  603.4 125.2 %all-to-all-start.8 = ((bf16[4,128,1536]{2,1,0:T(8,128)(2,1)}), bf16[4,128,1536]{2,1,0:T(8,128)(2,1)}, u32[]{:S(2)}, u32[]{:S(2)}) async-start(bf16[4,128,1536]{2,1,0:T(8,128)(2,1)} %bitcast.657), calls=%async_computation.8 | async-start | bytes 3145728 | tf_op jit(solution)/shard_map/all_to_all | solution.py:47
  608.6 372.8 %reduce-scatter.11.cloned.1.call-start = ((), (), s32[]{:S(2)}) async-start(), calls=%async_computation.17 | async-start | bytes 1511424 | tf_op jit(solution)/shard_map/reduce_scatter | solution.py:71
  (108 other events, 3481.0 us)
Sparse Core Ops, SparseCore 0:
  11.6 77.4 all-gather.8
  92.1 205.2 all-gather.10
  352.7 152.7 reduce-scatter.6
  511.5 170.4 all-reduce.8
  684.4 44.1 reduce-scatter.8
  734.1 221.8 reduce-scatter.12
  958.5 22.8 reduce-scatter.10
where the time goes:
time: 1000 us; the launch traced here: 993 us
  waiting for transfers between devices  408 us (41%)
  blocking collectives  241 us (24%)
  starting transfers between devices  105 us (10%)
  matrix products  102 us (10%)
  local copies, waits for them, and re-layouts  55.8 us (6%)
  other arithmetic  50.3 us (5%)
  between operations  21.5 us (2%)
    unnamed x9, waiting for transfers between devices  181 us
    all_gather x2, blocking collectives, over_pieces(): pieces = lax.all_gather(x, axis)  137 us
    all_to_all x1, blocking collectives, sum_at_owner(): pieces = lax.all_to_all(cut_along(x, dim, devices), axis, 0, 0, tiled=True)  81.6 us
    ppermute x20, starting transfers between devices, passed_along(): return lax.ppermute(block, axis, route)  68 us
    ppermute x20, waiting for transfers between devices, passed_along(): return lax.ppermute(block, axis, route)  66.6 us
    all_to_all x5, waiting for transfers between devices, from_everyone(): return lax.all_to_all(copies, axis, split_axis=0, concat_axis=0, tiled=True)  52.3 us
    reduce_scatter x3, waiting for transfers between devices, sum_by_axis(): running = lax.psum_scatter(running, axis, scatter_dimension=0, tiled=True)  51.8 us
    all_to_all x1, waiting for transfers between devices, sum_at_owner(): pieces = lax.all_to_all(cut_along(x, dim, devices), axis, 0, 0, tiled=True)  29.6 us
  transfers between devices with their start and end apart: 34, of which 22 were waited for; matrix products, arithmetic and copies ran while one was open for 15% of the time, Pallas kernels for 0%

commit v1 on v0

v1 whole, which is shorter than its diff:
```python
from functools import partial

import jax
import jax.numpy as jnp
from jax import lax
from jax.experimental import pallas as pl
from jax.experimental.pallas import tpu as pltpu
from jax.sharding import Mesh
from jax.sharding import PartitionSpec as P

EPS = 1e-05
THETA = 1000000.0
LOG2E = 1.4426950408889634
MESH = pl.DeviceIdType.MESH
BF = jnp.bfloat16
F32 = jnp.float32
HI = lax.Precision.HIGHEST
AXES = ("z", "y", "xh", "xl", "core")

D = 1536
HID = 864
HP = 896
CF = 3 * HP
CA = 512
ROWS = 1024
TILE = 256
NT = ((1,), (1,)), ((), ())
NN = ((1,), (0,)), ((), ())
TN = ((0,), (0,)), ((), ())


def mm(a, b, dims, precision=None):
    return lax.dot_general(a, b, dims, precision=precision, preferred_element_type=F32)


class Pos:
    def __init__(s):
        ax = lax.axis_index
        s.z, s.y, s.xh, s.xl, s.c = ax("z"), ax("y"), ax("xh"), ax("xl"), ax("core")
        s.x = s.xh * 2 + s.xl
        s.sb = s.z * 4 + s.y
        s.sib = s.at_x(0, 1 - s.c)

    def at_x(s, d, c=None):
        x = lax.rem(s.x + d, 4)
        return {"xh": x // 2, "xl": lax.rem(x, 2), "core": s.c if c is None else c}

    def at(s, axis, d):
        return {axis: lax.rem(getattr(s, axis) + d, 4)}

    def at_sb(s, d):
        t = lax.rem(s.sb + d + 16, 16)
        return {"z": t // 4, "y": lax.rem(t, 4)}


def barrier(p):
    b = pltpu.get_barrier_semaphore()
    peers = [p.at("y", 1), p.at("y", 2), p.at("y", 3), p.at("z", 1), p.at("z", 2), p.at("z", 3)]
    peers += [p.at_sb(d) for d in (1, 2, -1, -2)]
    peers += [p.at_x(d, cc) for d in (1, 2, 3) for cc in (p.c, 1 - p.c)] + [p.sib]
    for q in peers:
        pl.semaphore_signal(b, inc=1, device_id=q, device_id_type=MESH)
    pl.semaphore_wait(b, len(peers))


def rcopy(src, dst, ss, rs, dev):
    return pltpu.make_async_remote_copy(
        src_ref=src, dst_ref=dst, send_sem=ss, recv_sem=rs, device_id=dev, device_id_type=MESH
    )


def ds(start, n):
    return pl.ds(pl.multiple_of(start, 16), n)


class Half:
    def __init__(s, p, w, off, a, b, ss, rs):
        s.p, s.w, s.off, s.a, s.b, s.ss, s.rs = p, w, off, a, b, ss, rs
        s.sent = []

    def unit(s, ra, rb):
        ia = lax.rem(getattr(s.p, s.a) + ra, 4)
        ib = lax.rem(getattr(s.p, s.b) + rb, 4)
        zz, yy = (ia, ib) if s.a == "z" else (ib, ia)
        return s.w.at[ds((zz * 4 + yy) * 96 + s.off, 48)]

    def send(s, ra, rb, axis, d, rid):
        u = s.unit(ra, rb)
        k = rcopy(u, u, s.ss.at[len(s.sent)], s.rs.at[rid], s.p.at(axis, d))
        s.sent.append(k)
        k.start()

    def got(s, ra, rb, rid):
        u = s.unit(ra, rb)
        rcopy(u, u, s.ss.at[0], s.rs.at[rid], s.p.at(s.a, 1)).wait_recv()

    def own(s):
        s.send(0, 0, s.a, 1, 0)
        s.send(0, 0, s.a, 3, 1)
        s.send(0, 0, s.b, 1, 3)
        s.send(0, 0, s.b, 3, 7)

    def step(s, i):
        if i == 0:
            s.got(3, 0, 0)
            s.send(3, 0, s.a, 1, 2)
            s.send(3, 0, s.b, 1, 6)
            s.send(3, 0, s.b, 3, 10)
            s.got(1, 0, 1)
            s.send(1, 0, s.b, 1, 4)
            s.send(1, 0, s.b, 3, 8)
        if i == 1:
            s.got(0, 3, 3)
            s.send(0, 3, s.b, 1, 11)
            s.got(2, 0, 2)
            s.send(2, 0, s.b, 1, 5)
            s.send(2, 0, s.b, 3, 9)
        if i == 2:
            s.got(3, 1, 10)
            s.send(3, 1, s.b, 3, 14)
            s.got(1, 3, 4)
            s.send(1, 3, s.b, 1, 12)
        if i == 3:
            s.got(2, 1, 9)
            s.send(2, 1, s.b, 3, 13)
        if i == 4:
            s.got(0, 1, 7)
            s.got(1, 1, 8)
            s.got(2, 3, 5)
            s.got(3, 3, 6)
        if i == 5:
            for ra in range(4):
                s.got(ra, 2, 11 + ra)
            for k in s.sent:
                k.wait_send()


class Weights:
    def __init__(s, p, mine, theirs, w, xs, ls, ss, rs):
        s.p, s.mine, s.theirs, s.w, s.xs, s.ls = p, mine, theirs, w, xs, ls
        s.oo, s.po = p.xh * 48, (1 - p.xh) * 48
        s.A = Half(p, w, s.oo, "y", "z", ss.at[0], rs.at[0])
        s.B = Half(p, w, s.po, "z", "y", ss.at[1], rs.at[1])

    def exchange(s):
        p = s.p
        dst = s.w.at[ds(p.sb * 96 + s.oo, 48)]
        s.xk = rcopy(s.theirs, dst, s.xs.at[0], s.xs.at[1], p.at_x(2))
        s.xk.start()
        k = pltpu.make_async_copy(s.mine, dst, s.ls)
        k.start()
        k.wait()

    def own(s):
        p = s.p
        s.A.own()
        got = s.w.at[ds(p.sb * 96 + s.po, 48)]
        rcopy(s.theirs, got, s.xs.at[0], s.xs.at[1], p.at_x(2)).wait_recv()
        s.B.own()

    def step(s, i):
        s.A.step(i)
        s.B.step(i)
        if i == 5:
            s.xk.wait_send()


class GatherX:
    def __init__(s, p, buf, ss, rs):
        s.p, s.buf, s.ss, s.rs, s.sent = p, buf, ss, rs, []

    def shard(s, d, c, lo=0, n=128):
        x = lax.rem(s.p.x + d, 4)
        return s.buf.at[ds((x * 2 + c) * 128 + lo, n)]

    def send(s, d, lo, n, dev, rid):
        u = s.shard(d, s.p.c, lo, n)
        k = rcopy(u, u, s.ss.at[len(s.sent)], s.rs.at[rid], dev)
        s.sent.append(k)
        k.start()

    def got(s, d, c, lo, n, rid):
        u = s.shard(d, c, lo, n)
        rcopy(u, u, s.ss.at[0], s.rs.at[rid], s.p.at_x(1)).wait_recv()

    def own(s):
        p = s.p
        s.send(0, 0, 128, p.at_x(1), 0)
        s.send(0, 0, 128, p.at_x(3), 1)
        s.send(0, 0, 128, p.sib, 4)

    def step(s, i):
        p = s.p
        o = 1 - p.c
        if i == 0:
            s.got(3, p.c, 0, 128, 0)
            s.send(3, 0, 64, p.at_x(1), 2)
            s.send(3, 0, 128, p.sib, 5)
            s.got(1, p.c, 0, 128, 1)
            s.send(1, 64, 64, p.at_x(3), 3)
            s.send(1, 0, 128, p.sib, 6)
        if i == 1:
            s.got(2, p.c, 0, 64, 2)
            s.send(2, 0, 64, p.sib, 7)
            s.got(2, p.c, 64, 64, 3)
            s.send(2, 64, 64, p.sib, 8)
        if i == 2:
            s.got(0, o, 0, 128, 4)
        if i == 3:
            s.got(3, o, 0, 128, 5)
        if i == 4:
            s.got(1, o, 0, 128, 6)
        if i == 5:
            s.got(2, o, 0, 64, 7)
            s.got(2, o, 64, 64, 8)
            for k in s.sent:
                k.wait_send()


class ReduceX:
    def __init__(s, p, buf, sib, half, full, ss, rs):
        s.p, s.buf, s.sib, s.half, s.full, s.ss, s.rs, s.sent = p, buf, sib, half, full, ss, rs, []

    def rows(s, d, c, lo=0, n=128):
        x = lax.rem(s.p.x + d, 4)
        return ds((x * 2 + c) * 128 + lo, n)

    def send(s, src, dst, rid, dev):
        k = rcopy(src, dst, s.ss.at[rid], s.rs.at[rid], dev)
        s.sent.append(k)
        k.start()

    def wait(s, dst, rid):
        rcopy(dst, dst, s.ss.at[rid], s.rs.at[rid], s.p.sib).wait_recv()

    def to_sib(s, d):
        s.send(s.buf.at[s.rows(d, 1 - s.p.c)], s.sib.at[d], d, s.p.sib)

    def add_sib(s, d):
        s.wait(s.sib.at[d], d)
        r = s.rows(d, s.p.c)
        s.buf[r] = (s.buf[r].astype(F32) + s.sib[d].astype(F32)).astype(BF)

    def far(s):
        s.add_sib(2)
        s.send(s.buf.at[s.rows(2, s.p.c, 0, 64)], s.half.at[0], 4, s.p.at_x(1))
        s.send(s.buf.at[s.rows(2, s.p.c, 64, 64)], s.half.at[1], 5, s.p.at_x(3))

    def near(s):
        s.add_sib(1)
        s.add_sib(3)
        s.wait(s.half.at[0], 4)
        r = s.rows(1, s.p.c, 0, 64)
        s.buf[r] = (s.buf[r].astype(F32) + s.half[0].astype(F32)).astype(BF)
        s.send(s.buf.at[s.rows(1, s.p.c)], s.full.at[0], 6, s.p.at_x(1))
        s.wait(s.half.at[1], 5)
        r = s.rows(3, s.p.c, 64, 64)
        s.buf[r] = (s.buf[r].astype(F32) + s.half[1].astype(F32)).astype(BF)
        s.send(s.buf.at[s.rows(3, s.p.c)], s.full.at[1], 7, s.p.at_x(3))

    def final(s):
        s.wait(s.sib.at[0], 0)
        s.wait(s.full.at[0], 6)
        s.wait(s.full.at[1], 7)
        for k in s.sent:
            k.wait_send()
        r = s.rows(0, s.p.c)
        return (s.buf[r].astype(F32) + s.sib[0].astype(F32)) + (
            s.full[0].astype(F32) + s.full[1].astype(F32)
        )


class ReduceHalf:
    def __init__(s, p, g, off, a, b, rbuf, ss, rs):
        s.p, s.g, s.off, s.a, s.b, s.r, s.ss, s.rs = p, g, off, a, b, rbuf, ss, rs
        s.sent = []

    def rows(s, ra, rb):
        ia = lax.rem(getattr(s.p, s.a) + ra, 4)
        ib = lax.rem(getattr(s.p, s.b) + rb, 4)
        zz, yy = (ia, ib) if s.a == "z" else (ib, ia)
        return ds((zz * 4 + yy) * 96 + s.off, 48)

    def send(s, ra, rb, axis, d, rid):
        k = rcopy(s.g.at[s.rows(ra, rb)], s.r.at[rid], s.ss.at[len(s.sent)], s.rs.at[rid], s.p.at(axis, d))
        s.sent.append(k)
        k.start()

    def add(s, ra, rb, *rids):
        for i in rids:
            rcopy(s.r.at[i], s.r.at[i], s.ss.at[0], s.rs.at[i], s.p.at(s.a, 1)).wait_recv()
        r = s.rows(ra, rb)
        v = s.g[r].astype(F32)
        for i in rids:
            v = v + s.r[i].astype(F32)
        s.g[r] = v.astype(BF)

    def step(s, i):
        a, b = s.a, s.b
        if i == 0:
            for ra in (0, 1):
                s.send(ra, 2, b, 1, 11 + ra)
            for ra in (2, 3):
                s.send(ra, 2, b, 3, 11 + ra)
            for ra in (2, 3):
                s.send(ra, 1, b, 1, 3 + ra)
            for ra in (0, 1):
                s.send(ra, 3, b, 3, 7 + ra)
        if i == 1:
            for ra in (0, 1):
                s.add(ra, 1, 11 + ra)
                s.send(ra, 1, b, 1, 3 + ra)
            for ra in (2, 3):
                s.add(ra, 3, 11 + ra)
                s.send(ra, 3, b, 3, 7 + ra)
        if i == 2:
            s.add(2, 0, 5, 9)
            s.send(2, 0, a, 1, 2)
            s.add(3, 0, 6, 10)
            s.send(3, 0, a, 3, 1)
        if i == 3:
            s.add(1, 0, 4, 8, 2)
            s.send(1, 0, a, 1, 0)
        if i == 4:
            s.add(0, 0, 3, 7, 0, 1)
            for k in s.sent:
                k.wait_send()


class ReduceW:
    def __init__(s, p, g, rbuf, mine, other, xbuf, xs, ss, rs):
        s.p, s.g, s.mine, s.other, s.xbuf, s.xs = p, g, mine, other, xbuf, xs
        s.oo, s.po = p.xh * 48, (1 - p.xh) * 48
        s.A = ReduceHalf(p, g, s.oo, "y", "z", rbuf.at[0], ss.at[0], rs.at[0])
        s.B = ReduceHalf(p, g, s.po, "z", "y", rbuf.at[1], ss.at[1], rs.at[1])

    def step(s, i):
        p = s.p
        if i < 5:
            s.B.step(i)
        if i == 4:
            src = s.g.at[ds(p.sb * 96 + s.po, 48)]
            s.xk = rcopy(src, s.xbuf, s.xs.at[0], s.xs.at[1], p.at_x(2))
            s.xk.start()
        if i < 5:
            s.A.step(i)
        if i == 4:
            s.mine[...] = s.g[ds(p.sb * 96 + s.oo, 48)]
        if i == 5:
            s.xk.wait_recv()
            s.xk.wait_send()
            s.other[...] = s.xbuf[...]


def lanes(shape):
    return lax.broadcasted_iota(jnp.int32, shape, len(shape) - 1)


def swap(v):
    n = v.shape[1]
    low = lax.rem(lanes(v.shape), 64) < 32
    return jnp.where(low, pltpu.roll(v, n - 32, 1), pltpu.roll(v, 32, 1))


def head_mean(v):
    n = v.shape[1]
    a = lax.broadcasted_iota(jnp.int32, (n, n), 0) // 64
    b = lax.broadcasted_iota(jnp.int32, (n, n), 1) // 64
    m = jnp.where(a == b, 1.0 / 64, 0.0).astype(F32)
    return mm(v, m, NN, HI)


def rms_inv(v):
    return lax.rsqrt(jnp.mean(v * v, axis=-1, keepdims=True) + EPS)


def loop(n, body):
    lax.fori_loop(0, n, lambda i, c: (body(i), c)[1], 0)


def tile(t, n=TILE):
    return pl.ds(pl.multiple_of(t * n, n), n)


def kernel(
    tokens, segf, attn_gain, ffn_gain, gqk, wa_mine, wa_theirs, wf_mine, wf_theirs, out_grad, ctab, stab,
    result, grad_tokens, ga_mine, ga_other, gf_mine, gf_other, gains,
    wa, wf, bo, og, b2, mr, hid, dg, du, fr, ar, fx, axb,
    pa, psib, phalf, pfull,
    q, do, kvw, kvt, acc, dkv, dks, dkr, att, attf, qkraw, mid, dmid,
    segx, segw, stq, lse, dlt, gbuf, gx, gy, gz,
    wsx, wsl, was, war, wfs, wfr, gxs, gxr, rxs, rxr, ras, rar, rfs, rfr, kvs, kvr, sgs, sgr, gns, gnr, free,
):
    p = Pos()
    shard = p.x * 2 + p.c
    ga, dall = wa, dg
    own_rows = ds(shard * 128, 128)
    barrier(p)

    WA = Weights(p, wa_mine, wa_theirs, wa, wsx.at[0], wsl.at[0], was, war)
    WF = Weights(p, wf_mine, wf_theirs, wf, wsx.at[1], wsl.at[1], wfs, wfr)
    WA.exchange()
    tf = tokens[...].astype(F32)
    bo[own_rows] = (tf * rms_inv(tf) * attn_gain[...]).astype(BF)
    GB = GatherX(p, bo, gxs.at[0], gxr.at[0])
    GB.own()
    segx[pl.ds(pl.multiple_of(shard * 8, 8), 8)] = segf[...]
    seg_sent = []
    here = segx.at[pl.ds(pl.multiple_of(shard * 8, 8), 8)]
    peers = [(d, cc) for d in range(4) for cc in range(2) if (d, cc) != (0, 0)]
    for i, (d, cc) in enumerate(peers):
        k = rcopy(here, here, sgs.at[i], sgr.at[i], p.at_x(d, p.c if cc == 0 else 1 - p.c))
        k.start()
        seg_sent.append(k)
    WA.own()
    WF.exchange()
    for i, (d, cc) in enumerate(peers):
        x = lax.rem(p.x + 4 - d, 4)
        c = p.c if cc == 0 else 1 - p.c
        there = segx.at[pl.ds(pl.multiple_of((x * 2 + c) * 8, 8), 8)]
        rcopy(there, there, sgs.at[i], sgr.at[i], p.sib).wait_recv()
    for g in range(8):
        segw[pl.ds(16 + g, 1)] = segx[pl.ds(8 * g, 1)]
    for j in (1, 2):
        k = rcopy(segw.at[pl.ds(16, 8)], segw.at[pl.ds(16 - 8 * j, 8)], sgs.at[6 + j], sgr.at[6 + j], p.at_sb(j))
        k.start()
        seg_sent.append(k)
    og[own_rows] = out_grad[...]
    GB.step(0)
    WA.step(0)
    WA.step(1)
    GB.step(1)
    WA.step(2)
    GO = GatherX(p, og, gxs.at[1], gxr.at[1])
    WA.step(3)
    WF.own()
    for i in (2, 3, 4, 5):
        GB.step(i)
    WA.step(4)
    WA.step(5)
    GO.own()

    for j in (1, 2):
        there = segw.at[pl.ds(16 - 8 * j, 8)]
        rcopy(there, there, sgs.at[6 + j], sgr.at[6 + j], p.sib).wait_recv()
    for k in seg_sent:
        k.wait_send()
    sq = segw[pl.ds(16, 8)]
    s1 = jnp.where(p.sb >= 1, segw[pl.ds(8, 8)], -1.0)
    s2 = jnp.where(p.sb >= 2, segw[pl.ds(0, 8)], -1.0)
    start = jnp.zeros((8, 128), F32)
    for d in range(16):
        fewer = (sq < d).astype(F32) + (s1 < d).astype(F32) + (s2 < d).astype(F32)
        count = jnp.sum(jnp.sum(fewer, axis=1, keepdims=True), axis=0, keepdims=True)
        start = start + jnp.where(sq == d, count, 0.0)
    start = start.astype(jnp.int32)
    for t in range(4):
        for h in range(3):
            for j in range(2):
                stq[pl.ds(t, 1), pl.ds(h * 256 + j * 128, 128)] = start[2 * t + j : 2 * t + j + 1]

    def project(t):
        x = bo[tile(t)]
        qk = mm(x, wa[:, 0:256], NN)
        ov = mm(x, wa[:, 256:512], NN)
        qkraw[tile(t)] = qk
        n = qk * lax.rsqrt(head_mean(qk * qk) + EPS) * gqk[...]
        c1, s1 = ctab[tile(t)], stab[tile(t)]
        c2, s2 = jnp.concatenate([c1, c1], 1), jnp.concatenate([s1, s1], 1)
        r = n * c2 + swap(n) * s2
        a0, a1 = r[:, :128], r[:, 128:]
        low = lanes((TILE, 128)) < 64
        q[0, tile(t)] = jnp.where(low, a0, 0.0).astype(BF)
        q[1, tile(t)] = jnp.where(low, pltpu.roll(a0, 64, 1), 0.0).astype(BF)
        q[2, tile(t)] = jnp.where(low, a1, 0.0).astype(BF)
        kv = jnp.where(low, pltpu.roll(a1, 64, 1), ov[:, 128:])
        kvw[ds(2048 + t * 256, 256)] = kv.astype(BF)
        kvt[8 + t] = kv.T.astype(BF)

    loop(4, project)
    kv_own = kvw.at[pl.ds(2048, 1024)]
    kv_sent = []
    for j in (1, 2):
        k = rcopy(kv_own, kvw.at[pl.ds(2048 - 1024 * j, 1024)], kvs.at[j - 1], kvr.at[j - 1], p.at_sb(j))
        k.start()
        kv_sent.append(k)

    def kv_wait(j):
        there = kvw.at[pl.ds(2048 - 1024 * j, 1024)]
        rcopy(there, there, kvs.at[j - 1], kvr.at[j - 1], p.sib).wait_recv()

        def turn(t):
            u = 8 - 4 * j + t
            kvt[u] = kvw[tile(u)].astype(F32).T.astype(BF)

        loop(4, turn)

    key_at = lax.broadcasted_iota(jnp.int32, (TILE, 3 * TILE), 0)
    scale = 0.125

    def mask_of(t, u, diag):
        ok = key_at >= stq[pl.ds(t, 1)] - u * TILE
        if diag:
            ok = ok & (key_at <= lax.rem(lanes((TILE, 3 * TILE)), TILE))
        return ok

    def forward(t, u, diag):
        k = kvw[tile(u)]
        q3 = q[:, tile(t)].reshape(3 * TILE, 128)
        s = mm(k, q3, NT)
        e = jnp.where(mask_of(t, u, diag), jnp.exp2(s * (scale * LOG2E)), 0.0).astype(BF)
        va = jnp.where(lax.broadcasted_iota(jnp.int32, (128, TILE), 0) < 64, 1.0, kvt[u].astype(F32)).astype(BF)
        new = mm(va, e, NN)
        if diag:
            acc[t] = new
        else:
            acc[t] = acc[t] + new

    loop(4, lambda t: forward(t, t + 8, True))
    GO.step(0)
    WF.step(0)
    loop(3, lambda i: lax.fori_loop(0, i + 1, lambda j, c: (forward(i + 1, 8 + j, False), c)[1], 0))
    GO.step(1)
    kv_wait(1)
    WF.step(1)
    loop(4, lambda t: forward(t, 7, False))
    loop(4, lambda t: forward(t, 6, False))
    WF.step(2)
    loop(4, lambda t: forward(t, 5, False))
    loop(4, lambda t: forward(t, 4, False))
    for i in (2, 3, 4, 5):
        GO.step(i)
    kv_wait(2)
    WF.step(3)
    loop(4, lambda i: lax.fori_loop(0, i + 1, lambda t, c: (forward(t, i, False), c)[1], 0))
    for k in kv_sent:
        k.wait_send()

    def attended(t):
        a = acc[t]
        o = a[64:128] / a[0:64]
        lse[pl.ds(t, 1)] = jnp.log2(a[0:1])
        ot = jnp.concatenate([o[:, 0:256], o[:, 256:512], o[:, 512:768], jnp.zeros((64, 256), F32)], axis=0)
        o2 = ot.T
        attf[tile(t)] = o2
        att[tile(t)] = o2.astype(BF)

    loop(4, attended)

    R1 = ReduceX(p, pa, psib, phalf, pfull, rxs.at[0], rxr.at[0])
    for d in (2, 1, 3, 0):
        x = lax.rem(p.x + d, 4)
        for j in range(3):
            n = pl.ds(j * 512, 512)
            pa[tile(x), n] = mm(att[tile(x)], wa[n, 256:512], NT).astype(BF)
        R1.to_sib(d)
        if d == 1:
            R1.far()
    R1.near()
    WF.step(4)
    m = tokens[...].astype(F32) + R1.final()
    mid[...] = m
    b2[own_rows] = (m * rms_inv(m) * ffn_gain[...]).astype(BF)
    G2 = GatherX(p, b2, gxs.at[2], gxr.at[2])
    G2.own()
    WF.step(5)

    def ffn(d):
        r = tile(lax.rem(p.x + d, 4))
        for lo, n in ((0, 512), (512, HP - 512)):
            gate = mm(b2[r], wf[:, lo : lo + n], NN)
            up = mm(b2[r], wf[:, HP + lo : HP + lo + n], NN)
            dh = mm(og[r], wf[:, 2 * HP + lo : 2 * HP + lo + n], NN)
            sig = jax.nn.sigmoid(gate)
            swish = gate * sig
            hid[r, lo : lo + n] = (swish * up).astype(BF)
            dg[r, lo : lo + n] = (dh * up * sig * (1.0 + gate * (1.0 - sig))).astype(BF)
            du[r, lo : lo + n] = (dh * swish).astype(BF)

    G2.step(2)
    ffn(0)
    G2.step(0)
    G2.step(3)
    ffn(3)
    G2.step(1)
    G2.step(4)
    ffn(1)
    G2.step(5)
    ffn(2)

    R2 = ReduceX(p, pa, psib, phalf, pfull, rxs.at[1], rxr.at[1])
    R3 = ReduceX(p, pa, psib, phalf, pfull, rxs.at[2], rxr.at[2])

    def back_in(d):
        r = tile(lax.rem(p.x + d, 4))
        for j in range(3):
            n = pl.ds(j * 512, 512)
            v = mm(dg[r], wf[n, 0:HP], NT) + mm(du[r], wf[n, HP : 2 * HP], NT)
            pa[r, n] = v.astype(BF)
        R2.to_sib(d)

    def branch(d):
        r = tile(lax.rem(p.x + d, 4))
        for j in range(3):
            n = pl.ds(j * 512, 512)
            pa[r, n] = mm(hid[r], wf[n, 2 * HP :], NT).astype(BF)
        R3.to_sib(d)

    back_in(2)
    back_in(1)
    R2.far()
    back_in(3)
    back_in(0)
    R2.near()

    dn = R2.final()
    m = mid[...]
    r = rms_inv(m)
    n = m * r
    e = dn * ffn_gain[...]
    dm = out_grad[...].astype(F32) + r * (e - n * jnp.mean(e * n, axis=-1, keepdims=True))
    dmid[...] = dm
    gbuf[...] = jnp.zeros_like(gbuf)
    gbuf[pl.ds(1, 1)] = jnp.sum(dn * n, axis=0, keepdims=True)
    mr[own_rows] = dm.astype(BF)
    G3 = GatherX(p, mr, gxs.at[3], gxr.at[3])
    G3.own()

    def grads(cols, left, right):
        def body(i):
            c = pl.ds(pl.multiple_of(i * 256, 256), 256)
            wf[tile(i), cols] = mm(left[:, c], right[...], TN).astype(BF)

        loop(6, body)

    grads(pl.ds(0, HP), b2, dg)
    G3.step(0)
    grads(pl.ds(HP, HP), b2, du)
    G3.step(1)
    G3.step(2)
    branch(2)
    branch(1)
    R3.far()
    branch(3)
    branch(0)
    grads(pl.ds(2 * HP, HP), og, hid)
    RF = ReduceW(p, wf, fr, gf_mine, gf_other, fx, wsx.at[2], rfs, rfr)
    RF.step(0)
    for i in (3, 4, 5):
        G3.step(i)
    R3.near()

    head_row = lax.broadcasted_iota(jnp.int32, (8, 256), 0)
    head_lane = lanes((8, 256)) // 64
    per_head = jnp.where(head_row == head_lane, 1.0, 0.0).astype(F32)

    def d_attended(t):
        d = mm(mr[tile(t)], wa[:, 256:512], NN).astype(BF).astype(F32)
        sums = mm(per_head, d * attf[tile(t)], NT, HI)
        for h in range(3):
            dlt[pl.ds(t, 1), pl.ds(h * 256, 256)] = sums[h : h + 1]
        a0, a1 = d[:, :128], d[:, 128:]
        high = lanes((TILE, 128)) >= 64
        do[0, tile(t)] = jnp.where(high, pltpu.roll(a0, 64, 1), 0.0).astype(BF)
        do[1, tile(t)] = jnp.where(high, a0, 0.0).astype(BF)
        do[2, tile(t)] = jnp.where(high, pltpu.roll(a1, 64, 1), 0.0).astype(BF)
        acc[t] = jnp.zeros((128, 768), F32)

    loop(4, d_attended)
    result[...] = (mid[...] + R3.final()).astype(BF)
    for dev in (p.sib, p.at_x(1), p.at_x(3)):
        pl.semaphore_signal(free, inc=1, device_id=dev, device_id_type=MESH)
    dkv[...] = jnp.zeros_like(dkv)

    def backward(t, u, diag):
        k = kvw[tile(u)]
        q3 = q[:, tile(t)].reshape(3 * TILE, 128)
        do3 = do[:, tile(t)].reshape(3 * TILE, 128)
        s = mm(k, q3, NT)
        pr = jnp.where(mask_of(t, u, diag), jnp.exp2(s * (scale * LOG2E) - lse[pl.ds(t, 1)]), 0.0)
        dp = mm(k, do3, NT)
        dsc = (pr * (dp - dlt[pl.ds(t, 1)])).astype(BF)
        dkv[u] = dkv[u] + mm(dsc, q3, NN) + mm(pr.astype(BF), do3, NN)
        acc[t] = acc[t] + mm(kvt[u], dsc, NN)

    def scaled(v):
        return jnp.where(lanes(v.shape) < 64, v * scale, v)

    dk_sent = []

    def dk_send(j):
        def body(t):
            dks[j - 1, tile(t)] = scaled(dkv[8 - 4 * j + t]).astype(BF)

        loop(4, body)
        k = rcopy(dks.at[j - 1], dkr.at[j - 1], kvs.at[1 + j], kvr.at[1 + j], p.at_sb(-j))
        k.start()
        dk_sent.append(k)

    loop(4, lambda i: lax.fori_loop(0, i + 1, lambda t, c: (backward(t, i, False), c)[1], 0))
    dk_send(2)
    RF.step(1)
    loop(4, lambda t: backward(t, 4, False))
    loop(4, lambda t: backward(t, 5, False))
    RF.step(2)
    loop(4, lambda t: backward(t, 6, False))
    loop(4, lambda t: backward(t, 7, False))
    dk_send(1)
    RF.step(3)
    loop(3, lambda i: lax.fori_loop(0, i + 1, lambda j, c: (backward(i + 1, 8 + j, False), c)[1], 0))
    RF.step(4)
    loop(4, lambda t: backward(t, t + 8, True))
    for j in (1, 2):
        rcopy(dkr.at[j - 1], dkr.at[j - 1], kvs.at[1 + j], kvr.at[1 + j], p.sib).wait_recv()
    for k in dk_sent:
        k.wait_send()

    def unproject(t):
        a = acc[t][0:64]
        at = jnp.concatenate([a[:, 0:256], a[:, 256:512], a[:, 512:768], jnp.zeros((64, 256), F32)], axis=0)
        dq = at.T * scale
        dk = scaled(dkv[8 + t]) + dkr[0, tile(t)].astype(F32) + dkr[1, tile(t)].astype(F32)
        low = lanes((TILE, 128)) < 64
        d = jnp.concatenate([dq[:, :128], jnp.where(low, dq[:, 128:], pltpu.roll(dk, 64, 1))], 1)
        d = d.astype(BF).astype(F32)
        c1, s1 = ctab[tile(t)], stab[tile(t)]
        c2, s2 = jnp.concatenate([c1, c1], 1), jnp.concatenate([s1, s1], 1)
        dn = d * c2 + swap(d * s2)
        raw = qkraw[tile(t)]
        r = lax.rsqrt(head_mean(raw * raw) + EPS)
        n = raw * r
        e = dn * gqk[...]
        dx = r * (e - n * head_mean(e * n))
        gbuf[pl.ds(2, 1), pl.ds(0, 256)] = gbuf[pl.ds(2, 1), pl.ds(0, 256)] + jnp.sum(dn * n, axis=0, keepdims=True)
        dall[tile(t), 0:256] = dx.astype(BF)
        dall[tile(t), 256:384] = jnp.zeros((TILE, 128), BF)
        dall[tile(t), 384:512] = jnp.where(low, 0.0, dk).astype(BF)

    loop(4, unproject)

    pl.semaphore_wait(free, 3)
    R4 = ReduceX(p, pa, psib, phalf, pfull, rxs.at[3], rxr.at[3])
    for d in (2, 1, 3, 0):
        x = lax.rem(p.x + d, 4)
        for j in range(3):
            n = pl.ds(j * 512, 512)
            pa[tile(x), n] = mm(dall[tile(x), 0:512], wa[n, :], NT).astype(BF)
        R4.to_sib(d)
        if d == 1:
            R4.far()

    def attn_grads(i):
        c = pl.ds(pl.multiple_of(i * 256, 256), 256)
        ga[tile(i), 0:256] = mm(bo[:, c], dall[:, 0:256], TN).astype(BF)
        ga[tile(i), 256:512] = (mm(bo[:, c], dall[:, 256:512], TN) + mm(mr[:, c], att[...], TN)).astype(BF)

    loop(6, attn_grads)
    RA = ReduceW(p, ga, ar, ga_mine, ga_other, axb, wsx.at[3], ras, rar)
    RA.step(0)
    R4.near()
    RF.step(5)
    RA.step(1)
    dn = R4.final()
    t = tokens[...].astype(F32)
    r = rms_inv(t)
    n = t * r
    e = dn * attn_gain[...]
    grad_tokens[...] = (dmid[...] + r * (e - n * jnp.mean(e * n, axis=-1, keepdims=True))).astype(BF)
    gbuf[pl.ds(0, 1)] = jnp.sum(dn * n, axis=0, keepdims=True)
    RA.step(2)

    sent = []
    gx[shard] = gbuf[...]
    for i, (d, cc) in enumerate(peers):
        k = rcopy(gbuf, gx.at[shard], gns.at[i], gnr.at[i], p.at_x(d, p.c if cc == 0 else 1 - p.c))
        k.start()
        sent.append(k)
    RA.step(3)
    for i in range(7):
        rcopy(gx.at[i], gx.at[i], gns.at[i], gnr.at[i], p.sib).wait_recv()
    v = gx[0]
    for i in range(1, 8):
        v = v + gx[i]
    gy[p.y] = v
    for d in (1, 2, 3):
        k = rcopy(gy.at[p.y], gy.at[p.y], gns.at[6 + d], gnr.at[6 + d], p.at("y", d))
        k.start()
        sent.append(k)
    RA.step(4)
    for d in (1, 2, 3):
        rcopy(gy.at[0], gy.at[0], gns.at[6 + d], gnr.at[6 + d], p.sib).wait_recv()
    v = (gy[0] + gy[1]) + (gy[2] + gy[3])
    gz[p.z] = v
    for d in (1, 2, 3):
        k = rcopy(gz.at[p.z], gz.at[p.z], gns.at[9 + d], gnr.at[9 + d], p.at("z", d))
        k.start()
        sent.append(k)
    RA.step(5)
    for d in (1, 2, 3):
        rcopy(gz.at[0], gz.at[0], gns.at[9 + d], gnr.at[9 + d], p.sib).wait_recv()
    gains[...] = (gz[0] + gz[1]) + (gz[2] + gz[3])
    for k in sent:
        k.wait_send()


def call_kernel(*args):
    vm = pl.BlockSpec(memory_space=pltpu.VMEM)
    S = jax.ShapeDtypeStruct
    V = pltpu.VMEM
    dma = pltpu.SemaphoreType.DMA
    outs = (
        S((128, D), BF), S((128, D), BF), S((48, CA), BF), S((48, CA), BF),
        S((48, CF), BF), S((48, CF), BF), S((8, D), F32),
    )
    scratch = [
        V((D, CA), BF), V((D, CF), BF), V((ROWS, D), BF), V((ROWS, D), BF), V((ROWS, D), BF), V((ROWS, D), BF),
        V((ROWS, HP), BF), V((ROWS, HP), BF), V((ROWS, HP), BF),
        V((2, 15, 48, CF), BF), V((2, 15, 48, CA), BF), V((48, CF), BF), V((48, CA), BF),
        V((ROWS, D), BF), V((4, 128, D), BF), V((2, 64, D), BF), V((2, 128, D), BF),
        V((3, ROWS, 128), BF), V((3, ROWS, 128), BF), V((3 * ROWS, 128), BF), V((12, 128, TILE), BF),
        V((4, 128, 768), F32), V((12, TILE, 128), F32), V((2, ROWS, 128), BF), V((2, ROWS, 128), BF),
        V((ROWS, 256), BF), V((ROWS, 256), F32), V((ROWS, 256), F32),
        V((128, D), F32), V((128, D), F32),
        V((64, 128), F32), V((24, 128), F32), V((8, 768), jnp.int32), V((8, 768), F32), V((8, 768), F32),
        V((8, D), F32), V((8, 8, D), F32), V((4, 8, D), F32), V((4, 8, D), F32),
        dma((4, 2)), dma((2,)), dma((2, 15)), dma((2, 15)), dma((2, 15)), dma((2, 15)),
        dma((4, 9)), dma((4, 9)), dma((4, 8)), dma((4, 8)),
        dma((2, 15)), dma((2, 15)), dma((2, 15)), dma((2, 15)),
        dma((4,)), dma((4,)), dma((9,)), dma((9,)), dma((13,)), dma((13,)), pltpu.SemaphoreType.REGULAR,
    ]
    return pl.pallas_call(
        kernel,
        out_shape=outs,
        in_specs=[vm] * 5 + [pl.BlockSpec(memory_space=pl.ANY)] * 4 + [vm] * 3,
        out_specs=(vm,) * len(outs),
        scratch_shapes=scratch,
        compiler_params=pltpu.CompilerParams(
            collective_id=0, has_side_effects=True, vmem_limit_bytes=VMEM_LIMIT
        ),
    )(*args)


VMEM_LIMIT = 63 * 2**20


def on_device(
    tokens, segments, attn_gain, w_query, w_key, w_value, query_gain, key_gain, w_out, ffn_gain,
    w_gate, w_up, w_down, out_grad,
):
    xh = lax.axis_index("xh")
    sb = lax.axis_index("z") * 4 + lax.axis_index("y")

    wo, wd = w_out.T, w_down.T

    def attn_half(i):
        cut = lambda w, n: w[:, i * n : (i + 1) * n]
        return jnp.concatenate([cut(w_query, 192), cut(w_key, 64), cut(wo, 192), cut(w_value, 64)], axis=1)

    def ffn_half(i):
        cut = lambda w: jnp.pad(w[:, i * HID : (i + 1) * HID], ((0, 0), (0, HP - HID)))
        return jnp.concatenate([cut(w_gate), cut(w_up), cut(wd)], axis=1)

    def sides(of):
        a, b = of(0), of(1)
        return jnp.where(xh == 0, a, b), jnp.where(xh == 0, b, a)

    wa_mine, wa_theirs = sides(attn_half)
    wf_mine, wf_theirs = sides(ffn_half)
    steps = jnp.arange(32, dtype=F32) * (2.0 / 64)
    freqs = jnp.exp(-jnp.log(THETA) * steps)
    positions = (sb * ROWS + jnp.arange(ROWS, dtype=jnp.int32)).astype(F32)
    angles = positions[:, None] * freqs[None, :]
    cos, sin = jnp.cos(angles), jnp.sin(angles)
    ctab = jnp.concatenate([cos] * 4, axis=1)
    stab = jnp.concatenate([-sin, sin, -sin, sin], axis=1)
    gqk = jnp.concatenate([query_gain] * 3 + [key_gain])[None, :]
    segf = jnp.broadcast_to(segments.astype(F32)[None, :], (8, 128))

    result, grad_tokens, gam, gao, gfm, gfo, gains = call_kernel(
        tokens, segf, attn_gain[None], ffn_gain[None], gqk, wa_mine, wa_theirs, wf_mine, wf_theirs, out_grad, ctab, stab,
    )

    def both(mine, other):
        both = [jnp.where(xh == 0, mine, other), jnp.where(xh == 0, other, mine)]
        return jnp.concatenate(both, axis=1).astype(F32)

    ga = lambda lo, n: both(gam[:, lo : lo + n], gao[:, lo : lo + n])
    gf = lambda i: both(gfm[:, i * HP : i * HP + HID], gfo[:, i * HP : i * HP + HID])
    qg = gains[2, 0:64] + gains[2, 64:128] + gains[2, 128:192]
    return (
        result, grad_tokens, gains[0], ga(0, 192), ga(192, 64), ga(448, 64), qg, gains[2, 192:256],
        ga(256, 192).T, gains[1], gf(0), gf(1), gf(2).T,
    )


def solution(mesh):
    finer = Mesh(mesh.devices.reshape(4, 4, 2, 2, 2), AXES)
    rows, blk, narrow = P(AXES), ("z", "y", "xh"), ("xl", "core")
    cols, turned = P(blk, narrow), P(narrow, blk)
    in_specs = (rows, rows, P(), cols, cols, cols, P(), P(), turned, P(), cols, cols, turned, rows)
    out_specs = (rows, rows, P(), cols, cols, cols, P(), P(), turned, P(), cols, cols, turned)
    return jax.shard_map(
        on_device, mesh=finer, in_specs=in_specs, out_specs=out_specs, check_vma=False
    )
```

time: 1000 us -> 310 us (0.31)
  waiting for transfers between devices: 408 us -> 0 us
  Pallas kernels: 0 us -> 281 us
  blocking collectives: 241 us -> 0 us
  starting transfers between devices: 105 us -> 0 us
  matrix products: 102 us -> 0 us
  local copies, waits for them, and re-layouts: 55.8 us -> 7.39 us
  other arithmetic: 50.3 us -> 14 us
  between operations: 21.5 us -> 0.98 us
    pallas_call x0 -> x1, Pallas kernels: none -> 281 us  [call_kernel(): pl.pallas_call(kernel, out_shape=outs, in_specs=[vm] * 5 + [pl.BlockSpec(...]
    unnamed x9 -> x0, waiting for transfers between devices: 181 us -> none
    all_gather x2 -> x0, blocking collectives: 137 us -> none  [over_pieces(): pieces = lax.all_gather(x, axis)]
    all_to_all x2 -> x0, blocking collectives: 105 us -> none  [the longest x1 81.6 us: sum_at_owner(): pieces = lax.all_to_all(cut_along(x, dim, devices), axis, 0, 0, tiled=True)]
    dot_general x24 -> x0, matrix products: 102 us -> none  [the longest x1 10.9 us: on_device(): up = jnp.dot(block_two, wu_all, preferred_element_type=single_float)]
    all_to_all x7 -> x0, waiting for transfers between devices: 81.9 us -> none  [the longest x5 52.3 us: from_everyone(): return lax.all_to_all(copies, axis, split_axis=0, concat_axis=0, tiled=True)]
    ppermute x20 -> x0, starting transfers between devices: 68 us -> none  [passed_along(): return lax.ppermute(block, axis, route)]
    ppermute x20 -> x0, waiting for transfers between devices: 66.6 us -> none  [passed_along(): return lax.ppermute(block, axis, route)]
  transfers between devices with their start and end apart: 34 -> 0, of which waited for: 22 -> 0; matrix products, arithmetic and copies ran while one was open for 15% -> 0% of each run, Pallas kernels for 0% -> 0%
where the time goes in v1:
time: 310 us; the launch traced here: 304 us
  Pallas kernels  281 us (91%)
  other arithmetic  14 us (5%)
  local copies, waits for them, and re-layouts  7.39 us (2%)
    pallas_call x1, Pallas kernels, call_kernel(): pl.pallas_call(kernel, out_shape=outs, in_specs=[vm] * 5 + [pl.BlockSpec(...  281 us

profile of v1, /device:TPU:1, one launch (start us, length us, event | category | flops | bytes accessed | tf_op | source)
XLA Modules:
  0.0 303.8 jit_solution(709726785215502593)
XLA Ops:
  0.7 0.9 fusion.7
  1.7 0.7 broadcast_select_fusion.8
  2.4 1.9 fusion.6
  4.4 1.9 pad_maximum_fusion
  6.3 0.7 copy-done.11
  7.3 0.9 broadcast_select_fusion
  8.2 0.6 broadcast_in_dim.18.attn_gain
  8.9 0.6 broadcast_in_dim.19.ffn_gain
  9.5 0.6 broadcast_in_dim.8.segf
  10.2 0.6 pad_maximum_fusion.5
  10.8 281.4 %shard_map.237 = (bf16[128,1536]{1,0:T(8,128)(2,1)}, bf16[128,1536]{1,0:T(8,128)(2,1)}, bf16[48,512]{1,0:T(8,128)(2,1)}, bf16[48,512]{1,0:T(8,128)(2,1)}, bf16[4...) custom-call(bf16[128,1536]{1,0:T(8,128)(2,1)} %tokens.1, f32[8,128]{1,0:T(8,128)} %broadcast_in_dim.8.segf, ...), custom_call_target="tpu_custom_call" | custom-call | tf_op jit(solution)/shard_map/pallas_call | solution.py:831
  292.3 1.2 broadcast_select_fusion.3
  293.4 0.8 convert_bitcast_fusion
  294.3 0.8 maximum_convert_fusion.1
  295.1 0.8 maximum_convert_fusion
  296.0 0.7 convert_bitcast_fusion.1
  296.8 0.7 maximum_convert_fusion.4
  297.4 0.7 maximum_convert_fusion.3
  298.1 0.7 maximum_convert_fusion.2
  298.8 1.5 slice_reduce_fusion
  300.3 1.3 slice_bitcast_fusion
  301.7 0.7 copy.30
  302.4 0.4 copy-done
  302.8 0.7 copy.31
  (38 shorter events, 0.8 us)
Async XLA Ops:
  0.7 0.9 copy-start.7
  0.7 0.9 copy-start.8
  4.3 1.9 copy-start.2
  4.4 1.9 copy-start.3
  4.4 1.9 copy-start.4
  6.3 0.7 copy-start.11
  7.3 0.9 copy-start.9
  8.2 0.7 copy-start.10
  8.9 0.7 copy-start.14
  9.5 0.7 copy-start.12
  9.5 0.7 copy-start.13
  295.1 0.8 copy-start.5
  295.1 0.8 copy-start.6
  295.9 5.8 %copy-start.1 = (bf16[128,1536]{1,0:T(8,128)(2,1)S(1)}, bf16[128,1536]{1,0:T(8,128)(2,1)}, u32[]{:S(2)}) copy-start(bf16[128,1536]{1,0:T(8,128)(2,1)} %get-tuple-element.82) | copy-start | bytes 1179652
  301.7 1.1 copy-start
